TPU v7x, 512 devices: a whole 4x8x8 slice. The times are simulated.
512 devices in a mesh: aux: 32 (over x, z), occ: 16 (over y, core).
Axes of the slice: x: 4, y: 8, z: 8, core: 2. Of those that a mesh axis runs over, the one named last changes fastest.
Arguments:
- integrals: bfloat16 [12, 1024, 4096], P(None, 'aux'), may hold values from -5 to 5
- tile_pairs: int32 [32, 12, 2], P('aux'), may hold values from -1 to 15, as said below
- orbital_coef: bfloat16 [32, 16, 256], P(None, 'occ'), may hold values from -0.375 to 0.375
- domains: int32 [32, 16, 4], P(None, 'occ'), may hold values from 0 to 15, as said below
- occ_energy: bfloat16 [32, 16], P(None, 'occ'), may hold values from -1.5 to -0.29882812
- virt_energy: bfloat16 [16, 64], replicated, may hold values from 0.19921875 to 4
Outputs:
- amplitudes: bfloat16 [32, 16, 3, 1, 256, 256], P('aux', 'occ')
- pair_energy: float32 [32, 16, 3, 1], P('aux', 'occ')
Inputs may be any that keep to these rules, and one draw needn't show every extreme that they name: `tile_pairs`: each owner's live slots come first and name distinct tile pairs (t1, t2) inside one block of 4 consecutive tiles; the remaining slots hold -1 in both entries. Every owner has at least (12 + 2) // 3 live slots, some owner has all 12 live, and some owner has empty slots. `domains`: each orbital's domain is 4 consecutive tiles in increasing order.
All inputs are finite; a program needn't handle non-finite values.
Results may differ from a plain program's by a relative error of at most 0.005.
Values may be sent and summed in bfloat16 or wider, within the bound.
A program may use at most 64 MiB of HBM per device.

v0:
```python
import jax
import jax.numpy as jnp
from jax import lax
from jax.sharding import PartitionSpec as P

TILE = 64
DT = 4
OCC_DEV = 1
STEPS = 2


def passed_along(block, axis, distance):
    devices = range(lax.axis_size(axis))
    route = [((i - distance) % len(devices), i) for i in devices]
    return lax.ppermute(block, axis, route)


def half_transform(owner_ints, owner_pairs, coef, tiles):
    count, depth = tiles.shape
    rows = owner_ints.shape[1]
    coef_full = coef.astype(jnp.float32).reshape(count, depth, TILE)

    def slot_step(total, slot):
        block, pair = slot
        pick_first = (tiles == pair[0]).astype(jnp.float32)
        chosen = jnp.einsum("id,idm->im", pick_first, coef_full).astype(jnp.bfloat16)
        block_three = block.reshape(rows, TILE, TILE)
        partial_y = jnp.einsum(
            "im,pmn->pin", chosen, block_three, preferred_element_type=jnp.float32
        )
        pick_second = (tiles == pair[1]).astype(jnp.float32)
        return (total + jnp.einsum("id,pin->pidn", pick_second, partial_y), None)

    start = jnp.zeros((rows, count, depth, TILE), jnp.float32)
    total, _ = lax.scan(slot_step, start, (owner_ints, owner_pairs))
    return total.reshape(rows, count, depth * TILE).astype(jnp.bfloat16)


def domain_energy(tiles, virt_energy):
    onehot = (tiles[..., None] == jnp.arange(virt_energy.shape[0], dtype=jnp.int32)).astype(
        jnp.float32
    )
    table = jnp.einsum("...dt,tn->...dn", onehot, virt_energy.astype(jnp.float32))
    return table.reshape(tiles.shape[:-1] + (DT * TILE,)).astype(jnp.bfloat16)


def per_device(integrals, tile_pairs, orbital_coef, domains, occ_energy, virt_energy):
    owner_pairs = tile_pairs[0]
    owners = orbital_coef.shape[0]
    width = DT * TILE
    coef_list = [orbital_coef]
    energy_list = [occ_energy]
    tile_list = [domains]
    groups = len(coef_list)
    coef_all = jnp.stack(coef_list, axis=1)
    energy_all = jnp.stack(energy_list, axis=1)
    tiles_all = jnp.stack(tile_list, axis=1)
    count = owners * groups * OCC_DEV
    half = half_transform(
        integrals, owner_pairs, coef_all.reshape(count, width), tiles_all.reshape(count, DT)
    )
    half = half.reshape(half.shape[0], owners, groups * OCC_DEV, width)
    regrouped = lax.all_to_all(half, "aux", split_axis=1, concat_axis=0, tiled=True)
    place = lax.axis_index("aux")
    own_energy = lax.dynamic_index_in_dim(energy_all, place, 0, keepdims=False)
    own_tiles = lax.dynamic_index_in_dim(tiles_all, place, 0, keepdims=False)
    own_domain = domain_energy(own_tiles, virt_energy)
    own = (regrouped[:, 0], own_energy[0], own_domain[0])
    panels = [own]
    moving = own
    for step in range(STEPS):
        moving = passed_along((moving[0], moving[1], moving[2]), "occ", 1)
        panels.append(moving)
    mine_block, mine_energy, mine_domain = panels[0]
    mine_energy = mine_energy.astype(jnp.float32)
    mine_domain = mine_domain.astype(jnp.float32)
    amp_list = []
    pair_list = []
    for panel in panels:
        other_block, other_energy, other_domain = panel
        pair_int = jnp.einsum(
            "pia,pjb->ijab", mine_block, other_block, preferred_element_type=jnp.float32
        )
        denom = (
            mine_energy[:, None, None, None]
            + other_energy.astype(jnp.float32)[None, :, None, None]
            - mine_domain[:, None, :, None]
            - other_domain.astype(jnp.float32)[None, :, None, :]
        )
        ratio = pair_int / denom
        amp_list.append(ratio.astype(jnp.bfloat16))
        pair_list.append(jnp.sum(ratio * pair_int, axis=(2, 3)) / (width * width))
    amplitudes = jnp.stack(amp_list, axis=1)[None]
    pair_energy = jnp.stack(pair_list, axis=1)[None]
    return (amplitudes, pair_energy)


def solution(mesh):
    in_specs = (
        P(None, "aux", None),
        P("aux", None, None),
        P(None, "occ", None),
        P(None, "occ", None),
        P(None, "occ"),
        P(),
    )
    out_specs = (P("aux", "occ", None, None, None, None), P("aux", "occ", None, None))
    return jax.shard_map(
        per_device, mesh=mesh, in_specs=in_specs, out_specs=out_specs, check_vma=False
    )
```

profile of v0, /device:TPU:96, one launch (start us, length us, event | category | flops | bytes accessed | tf_op | source)
XLA Modules:
  0.0 131.7 jit_solution(360643793494642727)
XLA Ops:
  2.2 68.2 %while.11 = (s32[]{:T(128)}, f32[32,32,4,64]{3,2,1,0:T(4,128)S(1)}, s32[12,2]{0,1:T(2,128)}, s32[32,4]{1,0:T(8,128)S(1)}, bf16[32,4,64]{2,1,0:T(4,128)(2,1)S(1)}...) while((s32[]{:T(128)}, f32[32,32,4,64]{3,2,1,0:T(4,128)S(1)}, s32[12,2]{0,1:T(2,128)}, ...), condition=%wide.region_1.2_spmd.clone, body=%wide.region_0.1_spmd.clone.sunk | while | flops 9193859 | bytes 3966871 | solution.py:35
  3.5 1.3 compare_bitcast_fusion.2
  9.2 1.3 compare_bitcast_fusion.2
  12.4 1.2 bitcast_add_fusion.2
  14.9 1.3 compare_bitcast_fusion.2
  18.1 1.2 bitcast_add_fusion.2
  20.6 1.3 compare_bitcast_fusion.2
  23.8 1.2 bitcast_add_fusion.2
  26.3 1.3 compare_bitcast_fusion.2
  31.9 1.3 compare_bitcast_fusion.2
  35.1 1.2 bitcast_add_fusion.2
  37.6 1.3 compare_bitcast_fusion.2
  43.3 1.3 compare_bitcast_fusion.2
  49.0 1.3 compare_bitcast_fusion.2
  52.2 1.2 bitcast_add_fusion.2
  54.7 1.3 compare_bitcast_fusion.2
  60.3 1.3 compare_bitcast_fusion.2
  66.0 1.3 compare_bitcast_fusion.2
  69.2 1.2 bitcast_add_fusion.2
  71.9 30.0 %all_to_all.15 = bf16[32,32,1,256]{3,0,2,1:T(8,128)(2,1)S(1)} all-to-all(bf16[32,32,1,256]{3,0,2,1:T(8,128)(2,1)S(1)} %copy.16), channel_id=1, replica_groups=mesh['aux'=32,'occ'=16] {'aux'}, dimensions={1} | all-to-all | bytes 1048576 | tf_op jit(solution)/shard_map/all_to_all | solution.py:63
  105.1 6.8 %collective-permute-done.1 = bf16[1]{0:T(256)(128)(2,1)} collective-permute-done((bf16[1]{0:T(256)(128)(2,1)}, bf16[1]{0:T(256)(128)(2,1)}, u32[]{:S(2)}, u32[]{:S(2)}) %collective-permute-start.1) | collective-permute-done | bytes 34 | tf_op jit(solution)/shard_map/ppermute | solution.py:15
  113.1 4.2 %collective-permute-done.4 = bf16[1]{0:T(256)(128)(2,1)} collective-permute-done((bf16[1]{0:T(256)(128)(2,1)}, bf16[1]{0:T(256)(128)(2,1)}, u32[]{:S(2)}, u32[]{:S(2)}) %collective-permute-start.4) | collective-permute-done | bytes 34 | tf_op jit(solution)/shard_map/ppermute | solution.py:15
  118.7 4.1 %collective-permute-done.5 = bf16[1,256]{1,0:T(2,128)(2,1)S(1)} collective-permute-done((bf16[1,256]{1,0:T(2,128)(2,1)S(1)}, bf16[1,256]{1,0:T(2,128)(2,1)S(1)}, u32[]{:S(2)}, u32[]{:S(2)}) %collective-permute-start.5) | collective-permute-done | bytes 544 | tf_op jit(solution)/shard_map/ppermute | solution.py:15
  126.1 2.5 %collective-permute-done.3 = bf16[1024,1,256]{2,0,1:T(8,128)(2,1)S(1)} collective-permute-done((bf16[1024,1,256]{2,0,1:T(8,128)(2,1)S(1)}, bf16[1024,1,256]{2,0,1:T(8,128)(2,1)S(1)}, u32[]{:S(2)}, u32[]{:S(2)}) %collective-permute-start.3) | collective-permute-done | bytes 524320 | tf_op jit(solution)/shard_map/ppermute | solution.py:15
  (112 shorter events, 54.6 us)
Async XLA Ops:
  0.6 101.4 %copy-start = (bf16[16,64]{1,0:T(8,128)(2,1)S(1)}, bf16[16,64]{1,0:T(8,128)(2,1)}, u32[]{:S(2)}) copy-start(bf16[16,64]{1,0:T(8,128)(2,1)} %param.13) | copy-start | bytes 6148
  70.9 31.0 %copy-start.1 = (s32[32,1,4]{0,2,1:T(4,128)S(1)}, s32[32,1,4]{0,2,1:T(4,128)}, u32[]{:S(2)}) copy-start(s32[32,1,4]{0,2,1:T(4,128)} %param.11) | copy-start | bytes 1540
  70.9 32.2 %copy-start.2 = (bf16[32,1]{0,1:T(2,128)(2,1)S(1)}, bf16[32,1]{0,1:T(2,128)(2,1)}, u32[]{:S(2)}) copy-start(bf16[32,1]{0,1:T(2,128)(2,1)} %param.12) | copy-start | bytes 196
  101.9 16.8 %collective-permute-start = (bf16[1024,1,256]{2,0,1:T(8,128)(2,1)S(1)}, bf16[1024,1,256]{2,0,1:T(8,128)(2,1)S(1)}, u32[]{:S(2)}, u32[]{:S(2)}) collective-permute-start(bf16[1024,1,256]{2,0,1:T(8,128)(2,1)S(1)} %bitcast.98), channel_id=1, source_target_pairs={{15,0},{0,1},{1,2},{2,3},{3,4},{4,5},{5,6},{6,7},{7,8},{8,9},{9,10... | collective-permute-start | bytes 1572872 | tf_op jit(solution)/shard_map/ppermute | solution.py:15
  102.3 16.3 %collective-permute-start.2 = (bf16[1,256]{1,0:T(2,128)(2,1)S(1)}, bf16[1,256]{1,0:T(2,128)(2,1)S(1)}, u32[]{:S(2)}, u32[]{:S(2)}) collective-permute-start(bf16[1,256]{1,0:T(2,128)(2,1)S(1)} %convert_element_type.119), channel_id=1, source_target_pairs={{15,0},{0,1},{1,2},{2,3},{3,4},{4,5},{5,6},{6,7},{7,8},{8,9},{9,10... | collective-permute-start | bytes 1544 | tf_op jit(solution)/shard_map/ppermute | solution.py:15
  103.7 8.2 %collective-permute-start.1 = (bf16[1]{0:T(256)(128)(2,1)}, bf16[1]{0:T(256)(128)(2,1)}, u32[]{:S(2)}, u32[]{:S(2)}) collective-permute-start(bf16[1]{0:T(256)(128)(2,1)} %bitcast.8), channel_id=1, source_target_pairs={{15,0},{0,1},{1,2},{2,3},{3,4},{4,5},{5,6},{6,7},{7,8},{8,9},{9,10... | collective-permute-start | bytes 14 | tf_op jit(solution)/shard_map/ppermute | solution.py:15
  113.1 4.2 %collective-permute-start.4 = (bf16[1]{0:T(256)(128)(2,1)}, bf16[1]{0:T(256)(128)(2,1)}, u32[]{:S(2)}, u32[]{:S(2)}) collective-permute-start(bf16[1]{0:T(256)(128)(2,1)} %collective-permute-done.1), channel_id=1, source_target_pairs={{15,0},{0,1},{1,2},{2,3},{3,4},{4,5},{5,6},{6,7},{7,8},{8,9},{9,10... | collective-permute-start | bytes 14 | tf_op jit(solution)/shard_map/ppermute | solution.py:15
  118.6 4.2 %collective-permute-start.5 = (bf16[1,256]{1,0:T(2,128)(2,1)S(1)}, bf16[1,256]{1,0:T(2,128)(2,1)S(1)}, u32[]{:S(2)}, u32[]{:S(2)}) collective-permute-start(bf16[1,256]{1,0:T(2,128)(2,1)S(1)} %collective-permute-done.2), channel_id=1, source_target_pairs={{15,0},{0,1},{1,2},{2,3},{3,4},{4,5},{5,6},{6,7},{7,8},{8,9},{9,10... | collective-permute-start | bytes 1544 | tf_op jit(solution)/shard_map/ppermute | solution.py:15
  118.7 9.8 %collective-permute-start.3 = (bf16[1024,1,256]{2,0,1:T(8,128)(2,1)S(1)}, bf16[1024,1,256]{2,0,1:T(8,128)(2,1)S(1)}, u32[]{:S(2)}, u32[]{:S(2)}) collective-permute-start(bf16[1024,1,256]{2,0,1:T(8,128)(2,1)S(1)} %collective-permute-done), channel_id=1, source_target_pairs={{15,0},{0,1},{1,2},{2,3},{3,4},{4,5},{5,6},{6,7},{7,8},{8,9},{9,10... | collective-permute-start | bytes 1572872 | tf_op jit(solution)/shard_map/ppermute | solution.py:15
where the time goes:
time: 133 us; the launch traced here: 132 us
  local copies, waits for them, and re-layouts  37.9 us (28%)
  other arithmetic  30.6 us (23%)
  blocking collectives  30 us (23%)
  waiting for transfers between devices  17.5 us (13%)
  matrix products  7.56 us (6%)
  between operations  6.58 us (5%)
    all_to_all x1, blocking collectives, per_device(): lax.all_to_all(half, 'aux', split_axis=1, concat_axis=0, tiled=True)  30 us
    dynamic_slice x24, local copies, waits for them, and re-layouts, half_transform(): total, _ = lax.scan(slot_step, start, (owner_ints, owner_pairs))  20.7 us
    ppermute x6, waiting for transfers between devices, passed_along(): return lax.ppermute(block, axis, route)  17.5 us
    eq x12, other arithmetic, slot_step(): pick_first = (tiles == pair[0]).astype(jnp.float32)  15.2 us
    add x12, other arithmetic, slot_step(): return (total + jnp.einsum('id,pin->pidn', pick_second, partial_y), None)  14.3 us
    reshape x12, local copies, waits for them, and re-layouts, slot_step(): block_three = block.reshape(rows, TILE, TILE)  6.44 us
    slice x12, local copies, waits for them, and re-layouts, slot_step(): pick_first = (tiles == pair[0]).astype(jnp.float32)  6.33 us
    dot_general x3, matrix products, per_device(): jnp.einsum('pia,pjb->ijab', mine_block, other_block, preferred_element_ty...  2.86 us
  transfers between devices with their start and end apart: 6, of which 4 were waited for; matrix products, arithmetic and copies ran while one was open for 2% of the time, Pallas kernels for 0%

commit v1 on v0

v1 whole, which is shorter than its diff:
```python
import jax
import jax.numpy as jnp
from jax import lax
from jax.experimental import pallas as pl
from jax.experimental.pallas import tpu as pltpu
from jax.sharding import PartitionSpec as P

TILE = 64
DT = 4
NBT = 16
NPT = 12
AUX_DEV = 32
N_AUX = 32
NX = 4
NZ = 8
N_OCC = 16
WIDTH = DT * TILE
STEPS = 2
MP = TILE // 2
DEPTH = NPT * MP
HALF = 16
PARTS = AUX_DEV // HALF
GROUPS = 4
PER = N_AUX // GROUPS
MESH = pl.DeviceIdType.MESH
f32 = jnp.float32
bf16 = jnp.bfloat16


def kernel(
    ints_ref, pairs_ref, tiles_smem, coef_ref, tiles_ref, occ_ref, virt_ref,
    amp_ref, energy_ref,
    raw, rows, turned, outbox, own, next1, next2, chosen, level, level1, level2, inverse, total,
    load_sem, own_sem, send_sem, recv_sem, fwd_sem, fwd2_sem, n1_sem, n2_sem, lvl_send, lvl_recv,
):
    me = lax.axis_index("aux")
    occ = lax.axis_index("occ")
    my_x, my_z = me // NZ, me % NZ
    even = occ % 2 == 0

    def at_offset(k, sign):
        dx, dz = k // NZ, k % NZ
        return ((my_x + sign * dx + NX) % NX) * NZ + (my_z + sign * dz + NZ) % NZ

    def at_occ(step):
        return (me, (occ + step + N_OCC) % N_OCC)

    def load(part, third):
        s = third * 4
        return pltpu.make_async_copy(
            ints_ref.at[pl.ds(s, 4), pl.ds(part * HALF, HALF)],
            raw.at[pl.ds(s, 4), pl.ds(part * HALF, HALF)],
            load_sem.at[part, third],
        )

    for part in range(PARTS):
        for third in range(3):
            load(part, third).start()

    barrier = pltpu.get_barrier_semaphore()

    def greet(k, carry):
        pl.semaphore_signal(barrier, inc=1, device_id=(at_offset(k, 1), occ), device_id_type=MESH)
        return carry

    lax.fori_loop(1, N_AUX, greet, 0)
    for step in (1, 2, -1, -2):
        pl.semaphore_signal(barrier, inc=1, device_id=at_occ(step), device_id_type=MESH)

    coef = coef_ref[...]
    lane = lax.broadcasted_iota(jnp.int32, (WIDTH, 128), 1) % MP
    row = lax.broadcasted_iota(jnp.int32, (WIDTH, 128), 0)
    slot_of = lax.broadcasted_iota(jnp.int32, (1, DEPTH), 1) // MP
    first = jnp.full((1, DEPTH), -1, jnp.int32)
    second = jnp.full((1, DEPTH), -1, jnp.int32)
    for s in range(NPT):
        first = jnp.where(slot_of == s, pairs_ref[0, s, 0], first)
        second = jnp.where(slot_of == s, pairs_ref[0, s, 1], second)
    tiles = tiles_ref[...]
    for parity in range(2):
        picked = jnp.zeros((N_AUX, DEPTH), f32)
        for d in range(DT):
            spread = (row == d * TILE + 2 * lane + parity).astype(f32).astype(bf16)
            values = jnp.dot(coef, spread, preferred_element_type=f32)
            values = jnp.concatenate([values] * (DEPTH // 128), axis=1)
            picked = jnp.where(tiles[:, d : d + 1] == first, values, picked)
        for d in range(DT):
            part_rows = jnp.where(tiles[:, d : d + 1] == second, picked, 0.0)
            start = parity * 128 + (d % 2) * 64 + (d // 2) * 32
            chosen[start : start + 32, :] = part_rows.astype(bf16)

    virt = virt_ref[...].astype(f32)
    tile_row = lax.broadcasted_iota(jnp.int32, (NBT, TILE), 0)
    pieces = []
    for d in range(DT):
        mine = tiles_smem[me, 0, d]
        pieces.append(jnp.sum(jnp.where(tile_row == mine, virt, 0.0), axis=0, keepdims=True))
    domain = jnp.concatenate(pieces, axis=1)
    occ_row = lax.broadcasted_iota(jnp.int32, (N_AUX, 1), 0)
    occupied = jnp.sum(jnp.where(occ_row == me, occ_ref[...].astype(f32), 0.0), axis=0, keepdims=True)
    level[...] = jnp.broadcast_to(occupied - domain, (8, WIDTH))

    low_half = lax.broadcasted_iota(jnp.int32, (64, 128), 1) < TILE

    def transform(part):
        for third in range(3):
            load(part, third).wait()

        def spread_rows(s, carry):
            for mp in range(MP):
                base = pl.multiple_of((s * MP + mp) * HALF, HALF)
                rows[pl.ds(base, HALF), :] = raw[
                    s, part * HALF : (part + 1) * HALF, mp * 128 : (mp + 1) * 128
                ].astype(f32)
            return carry

        lax.fori_loop(0, NPT, spread_rows, 0)
        matrix = chosen[...]
        for p in range(0, HALF, 2):
            panel = jnp.concatenate(
                [rows[pl.ds(p + i, DEPTH, stride=HALF), :].astype(bf16) for i in range(2)], axis=1
            )
            product = jnp.dot(matrix, panel, preferred_element_type=f32)
            for i in range(2):
                c = slice(i * 128, (i + 1) * 128)
                straight = jnp.where(low_half, product[0:64, c], product[192:256, c])
                crossed = jnp.where(low_half, product[64:128, c], product[128:192, c])
                turned[(p + i) * 64 : (p + i + 1) * 64, :] = straight + pltpu.roll(crossed, TILE, 1)
        for r in range(N_AUX):
            for pair in range(2):
                block = turned[pl.ds(pair * 32 + r, HALF, stride=64), :]
                outbox[
                    r, part * HALF : (part + 1) * HALF, pair * 128 : (pair + 1) * 128
                ] = block.astype(bf16)

    def send(k, part):
        to = at_offset(k, -1)
        return pltpu.make_async_remote_copy(
            src_ref=outbox.at[to, pl.ds(part * HALF, HALF)],
            dst_ref=own.at[k, pl.ds(part * HALF, HALF)],
            send_sem=send_sem.at[k, part],
            recv_sem=recv_sem.at[k, part],
            device_id=(to, occ),
            device_id_type=MESH,
        )

    def start_sends(part):
        def one(k, carry):
            send(k, part).start()
            return carry

        lax.fori_loop(1, N_AUX, one, 0)

    def pass_level(step, target):
        return pltpu.make_async_remote_copy(
            src_ref=level, dst_ref=target, send_sem=lvl_send.at[step - 1], recv_sem=lvl_recv.at[step - 1],
            device_id=at_occ(step), device_id_type=MESH,
        )

    def to_next(k):
        return pltpu.make_async_remote_copy(
            src_ref=own.at[k], dst_ref=next1.at[k], send_sem=fwd_sem.at[k], recv_sem=n1_sem.at[k],
            device_id=at_occ(1), device_id_type=MESH,
        )

    def to_second(k):
        return pltpu.make_async_remote_copy(
            src_ref=own.at[k], dst_ref=next2.at[k], send_sem=fwd2_sem.at[0, k], recv_sem=n2_sem.at[k],
            device_id=at_occ(2), device_id_type=MESH,
        )

    def relay(k):
        return pltpu.make_async_remote_copy(
            src_ref=next1.at[k], dst_ref=next2.at[k], send_sem=fwd2_sem.at[1, k], recv_sem=n2_sem.at[k],
            device_id=at_occ(1), device_id_type=MESH,
        )

    def pass_on(k):
        to_next(k).start()

        @pl.when(even)
        def _():
            to_second(k).start()

    transform(0)
    pl.semaphore_wait(barrier, N_AUX - 1 + 4)
    pass_level(1, level1).start()
    pass_level(2, level2).start()
    start_sends(0)
    transform(1)
    start_sends(1)
    keep = pltpu.make_async_copy(outbox.at[me], own.at[0], own_sem)
    keep.start()

    pass_level(1, level1).wait()
    pass_level(2, level2).wait()
    column = jnp.transpose(jnp.broadcast_to(level[0:1, :], (WIDTH, WIDTH)))
    for g, other in enumerate((level, level1, level2)):
        inverse[g] = 1.0 / (column + other[0:1, :])
    keep.wait()

    def add(g, group, ref):
        k0 = group * PER
        left = own[k0 : k0 + PER].reshape(PER * AUX_DEV, WIDTH)
        right = ref[k0 : k0 + PER].reshape(PER * AUX_DEV, WIDTH)
        product = lax.dot_general(left, right, (((0,), (0,)), ((), ())), preferred_element_type=f32)
        if group == 0:
            total[g] = product
        else:
            total[g] += product

    def take_own(k, carry):
        for part in range(PARTS):
            send(k, part).wait_recv()
        pass_on(k)
        return carry

    def take_next(k, carry):
        to_next(k).wait_recv()

        @pl.when(even)
        def _():
            relay(k).start()

        return carry

    def take_second(k, carry):
        to_second(k).wait_recv()
        return carry

    pass_on(0)
    for group in range(GROUPS):
        lax.fori_loop(max(1, group * PER), (group + 1) * PER, take_own, 0)
        add(0, group, own)
        if group >= 1:
            lax.fori_loop((group - 1) * PER, group * PER, take_next, 0)
            add(1, group - 1, next1)
        if group >= 2:
            lax.fori_loop((group - 2) * PER, (group - 1) * PER, take_second, 0)
            add(2, group - 2, next2)

    def drain(k, carry):
        for part in range(PARTS):
            send(k, part).wait_send()
        return carry

    lax.fori_loop(1, N_AUX, drain, 0)
    last = GROUPS - 1
    lax.fori_loop(last * PER, N_AUX, take_next, 0)
    add(1, last, next1)
    lax.fori_loop((last - 1) * PER, last * PER, take_second, 0)
    add(2, last - 1, next2)

    def finish(g):
        value = total[g]
        ratio = value * inverse[g]
        amp_ref[g] = ratio.astype(bf16)
        energy_ref[0, g] = jnp.sum(ratio * value) / (WIDTH * WIDTH)

    finish(0)
    finish(1)

    def drain_forward(k, carry):
        to_next(k).wait_send()

        @pl.when(even)
        def _():
            to_second(k).wait_send()
            relay(k).wait_send()

        return carry

    lax.fori_loop(last * PER, N_AUX, take_second, 0)
    add(2, last, next2)
    finish(2)
    lax.fori_loop(0, N_AUX, drain_forward, 0)


def per_device(integrals, tile_pairs, orbital_coef, domains, occ_energy, virt_energy):
    vmem = pl.BlockSpec(memory_space=pltpu.VMEM)
    smem = pl.BlockSpec(memory_space=pltpu.SMEM)
    amps, energies = pl.pallas_call(
        kernel,
        out_shape=(
            jax.ShapeDtypeStruct((STEPS + 1, WIDTH, WIDTH), bf16),
            jax.ShapeDtypeStruct((1, STEPS + 1), f32),
        ),
        in_specs=[pl.BlockSpec(memory_space=pl.ANY), smem, smem, vmem, vmem, vmem, vmem],
        out_specs=(vmem, smem),
        scratch_shapes=[
            pltpu.VMEM((NPT, AUX_DEV, TILE * TILE), bf16),
            pltpu.VMEM((DEPTH * HALF, 128), f32),
            pltpu.VMEM((HALF * 64, 128), f32),
            pltpu.VMEM((N_AUX, AUX_DEV, WIDTH), bf16),
            pltpu.VMEM((N_AUX, AUX_DEV, WIDTH), bf16),
            pltpu.VMEM((N_AUX, AUX_DEV, WIDTH), bf16),
            pltpu.VMEM((N_AUX, AUX_DEV, WIDTH), bf16),
            pltpu.VMEM((256, DEPTH), bf16),
            pltpu.VMEM((8, WIDTH), f32),
            pltpu.VMEM((8, WIDTH), f32),
            pltpu.VMEM((8, WIDTH), f32),
            pltpu.VMEM((STEPS + 1, WIDTH, WIDTH), f32),
            pltpu.VMEM((STEPS + 1, WIDTH, WIDTH), f32),
            pltpu.SemaphoreType.DMA((PARTS, 3)),
            pltpu.SemaphoreType.DMA,
            pltpu.SemaphoreType.DMA((N_AUX, PARTS)),
            pltpu.SemaphoreType.DMA((N_AUX, PARTS)),
            pltpu.SemaphoreType.DMA((N_AUX,)),
            pltpu.SemaphoreType.DMA((2, N_AUX)),
            pltpu.SemaphoreType.DMA((N_AUX,)),
            pltpu.SemaphoreType.DMA((N_AUX,)),
            pltpu.SemaphoreType.DMA((2,)),
            pltpu.SemaphoreType.DMA((2,)),
        ],
        compiler_params=pltpu.CompilerParams(
            collective_id=0, has_side_effects=True, vmem_limit_bytes=40 << 20
        ),
    )(
        integrals,
        tile_pairs,
        domains,
        orbital_coef.reshape(N_AUX, WIDTH),
        domains.reshape(N_AUX, DT),
        occ_energy,
        virt_energy,
    )
    return (
        amps.reshape(1, 1, STEPS + 1, 1, WIDTH, WIDTH),
        energies.reshape(1, 1, STEPS + 1, 1),
    )


def solution(mesh):
    in_specs = (
        P(None, "aux", None),
        P("aux", None, None),
        P(None, "occ", None),
        P(None, "occ", None),
        P(None, "occ"),
        P(),
    )
    out_specs = (P("aux", "occ", None, None, None, None), P("aux", "occ", None, None))
    return jax.shard_map(
        per_device, mesh=mesh, in_specs=in_specs, out_specs=out_specs, check_vma=False
    )
```

time: 133 us -> 51.1 us (0.38)
  the two profiles are of different devices: /device:TPU:96 before, /device:TPU:1 now
where the time goes in v1:
time: 51.1 us; the launch traced here: 50.8 us
  Pallas kernels  42.6 us (83%)
  local copies, waits for them, and re-layouts  7.59 us (15%)
  between operations  0.64 us (1%)
    pallas_call x1, Pallas kernels, per_device(): pl.pallas_call(kernel, out_shape=(jax.ShapeDtypeStruct((STEPS + 1, WIDTH,...  42.6 us
    unnamed x11, local copies, waits for them, and re-layouts  6.83 us

profile of v1, /device:TPU:1, one launch (start us, length us, event | category | flops | bytes accessed | tf_op | source)
XLA Modules:
  0.0 50.8 jit_solution(14803707002940056010)
XLA Ops:
  0.6 0.8 %copy.8.pairs_ref = s32[1,12,2]{2,1,0:T(8,128)S(1)} copy(s32[1,12,2]{1,2,0:T(2,128)} %param.7) | data formatting | bytes 192 | tf_op args[1]
  1.4 0.7 %copy.11.occ_ref = bf16[32,1]{1,0:T(8,128)(2,1)S(1)} copy(bf16[32,1]{0,1:T(2,128)(2,1)} %param.10) | data formatting | bytes 128 | tf_op args[4]
  2.1 0.8 %copy.10.tiles_ref = s32[32,4]{1,0:T(8,128)S(1)} copy(s32[32,4]{0,1:T(4,128)} %bitcast.9) | data formatting | bytes 1024 | tf_op jit(solution)/shard_map/reshape | solution.py:323
  2.9 0.8 %copy.9.tiles_smem = s32[32,1,4]{2,1,0:T(1,128)S(1)} copy(s32[32,1,4]{0,2,1:T(4,128)} %param.9) | data formatting | bytes 1024 | tf_op args[3]
  3.7 0.0 copy-start
  3.7 1.9 %copy-done = bf16[12,32,4096]{2,1,0:T(8,128)(2,1)S(1)} copy-done((bf16[12,32,4096]{2,1,0:T(8,128)(2,1)S(1)}, bf16[12,32,4096]{2,1,0:T(8,128)(2,1)}, u32[]{:S(2)}) %copy-start) | copy-done | bytes 3145752
  5.6 0.0 copy-start.1
  5.6 0.7 %copy-done.1 = bf16[32,1,256]{2,0,1:T(8,128)(2,1)S(1)} copy-done((bf16[32,1,256]{2,0,1:T(8,128)(2,1)S(1)}, bf16[32,1,256]{2,0,1:T(8,128)(2,1)}, u32[]{:S(2)}) %copy-start.1) | copy-done | bytes 16408
  6.3 0.0 copy-start.2
  6.3 0.7 %copy-done.2 = bf16[16,64]{1,0:T(8,128)(2,1)S(1)} copy-done((bf16[16,64]{1,0:T(8,128)(2,1)S(1)}, bf16[16,64]{1,0:T(8,128)(2,1)}, u32[]{:S(2)}) %copy-start.2) | copy-done | bytes 2072
  7.0 42.6 %shard_map.77 = (bf16[3,256,256]{2,1,0:T(8,128)(2,1)S(1)}, f32[1,3]{1,0:T(1,128)S(1)}) custom-call(bf16[12,32,4096]{2,1,0:T(8,128)(2,1)S(1)} %copy-done, s32[1,12,2]{2,1,0:T(8,128)S(1)} %copy.8.pairs_ref, s32[32,1,4]{2,1,0:T(1,128)S(1)} %copy.9.tiles_smem, bf16[32,256]{1,0:T(8,128)(2,1)S(1)} %bitcast.7, s32[32,4]{1,0:T(8,128)S(1)} %copy.10.tiles_ref, ...), custom_call_target="tpu_custom_call" | custom-call | tf_op jit(solution)/shard_map/pallas_call | solution.py:282
  49.6 0.7 %copy.15 = bf16[1,1,3,1,256,256]{5,4,3,2,1,0:T(8,128)(2,1)} copy(bf16[1,1,3,1,256,256]{5,4,3,2,1,0:T(8,128)(2,1)S(1)} %bitcast.6) | data formatting | bytes 786432
  50.3 0.5 %copy.16 = f32[1,1,3,1]{2,3,1,0:T(1,128)} copy(f32[1,1,3,1]{2,3,1,0:T(1,128)S(1)} %bitcast.8) | data formatting | bytes 24
Async XLA Ops:
  3.7 1.9 %copy-start = (bf16[12,32,4096]{2,1,0:T(8,128)(2,1)S(1)}, bf16[12,32,4096]{2,1,0:T(8,128)(2,1)}, u32[]{:S(2)}) copy-start(bf16[12,32,4096]{2,1,0:T(8,128)(2,1)} %ints_ref.1) | copy-start | bytes 9437188
  5.6 0.7 %copy-start.1 = (bf16[32,1,256]{2,0,1:T(8,128)(2,1)S(1)}, bf16[32,1,256]{2,0,1:T(8,128)(2,1)}, u32[]{:S(2)}) copy-start(bf16[32,1,256]{2,0,1:T(8,128)(2,1)} %param.8) | copy-start | bytes 49156
  6.3 0.7 %copy-start.2 = (bf16[16,64]{1,0:T(8,128)(2,1)S(1)}, bf16[16,64]{1,0:T(8,128)(2,1)}, u32[]{:S(2)}) copy-start(bf16[16,64]{1,0:T(8,128)(2,1)} %virt_ref.1) | copy-start | bytes 6148

commit v2 on v1

v2 whole, which is shorter than its diff:
```python
import jax
import jax.numpy as jnp
from jax import lax
from jax.experimental import pallas as pl
from jax.experimental.pallas import tpu as pltpu
from jax.sharding import PartitionSpec as P

TILE = 64
DT = 4
NBT = 16
NPT = 12
AUX_DEV = 32
N_AUX = 32
NX = 4
NZ = 8
N_OCC = 16
WIDTH = DT * TILE
STEPS = 2
MP = TILE // 2
DEPTH = NPT * MP
HALF = 16
PARTS = AUX_DEV // HALF
BUNCH = 4
BUNCHES = N_AUX // BUNCH
LAG = 4
MESH = pl.DeviceIdType.MESH
f32 = jnp.float32
bf16 = jnp.bfloat16


def kernel(
    ints_ref, pairs_hbm, coef_hbm, tiles_hbm, occ_hbm, virt_hbm,
    amp_ref, energy_ref,
    pairs_ref, coef_ref, tiles_ref, occ_ref, virt_ref,
    raw, rows, turned, outbox, own, next1, next2, chosen, level, level1, level2, inverse, total,
    small_sem, load_sem, own_sem, send_sem, recv_sem, fwd_sem, n1_sem, n2_sem, lvl_send, lvl_recv,
):
    me = lax.axis_index("aux")
    occ = lax.axis_index("occ")
    my_x, my_z = me // NZ, me % NZ
    even = occ % 2 == 0

    x_at = [lax.rem(my_x + NX - dx, NX) * NZ for dx in range(NX)]
    z_at = [lax.rem(my_z + NZ - dz, NZ) for dz in range(NZ)]

    def behind(k):
        return x_at[k // NZ] + z_at[k % NZ]

    def at_occ(step):
        return (me, (occ + step + N_OCC) % N_OCC)

    barrier = pltpu.get_barrier_semaphore()

    for k in range(1, N_AUX):
        pl.semaphore_signal(barrier, inc=1, device_id=(behind(k), occ), device_id_type=MESH)
    for step in (1, 2, -1, -2):
        pl.semaphore_signal(barrier, inc=1, device_id=at_occ(step), device_id_type=MESH)

    def load(part, third):
        s = third * 4
        return pltpu.make_async_copy(
            ints_ref.at[pl.ds(s, 4), pl.ds(part * HALF, HALF)],
            raw.at[pl.ds(s, 4), pl.ds(part * HALF, HALF)],
            load_sem.at[part, third],
        )

    small = [
        pltpu.make_async_copy(src, dst, small_sem.at[i])
        for i, (src, dst) in enumerate((
            (coef_hbm, coef_ref), (tiles_hbm, tiles_ref), (pairs_hbm, pairs_ref),
            (occ_hbm, occ_ref), (virt_hbm, virt_ref),
        ))
    ]
    for copy in small:
        copy.start()
    for part in range(PARTS):
        for third in range(3):
            load(part, third).start()

    for copy in small:
        copy.wait()

    coef = coef_ref[...]
    lane = lax.broadcasted_iota(jnp.int32, (WIDTH, 128), 1) % MP
    row = lax.broadcasted_iota(jnp.int32, (WIDTH, 128), 0)
    slot_of = lax.broadcasted_iota(jnp.int32, (1, DEPTH), 1) // MP
    pairs = pairs_ref[...]
    first = jnp.full((1, DEPTH), -1, jnp.int32)
    second = jnp.full((1, DEPTH), -1, jnp.int32)
    for s in range(NPT):
        first = jnp.where(slot_of == s, pairs[0:1, s : s + 1], first)
        second = jnp.where(slot_of == s, pairs[1:2, s : s + 1], second)
    tiles = tiles_ref[...]
    diagonal = lax.broadcasted_iota(jnp.int32, (N_AUX, N_AUX), 0) == lax.broadcasted_iota(
        jnp.int32, (N_AUX, N_AUX), 1
    )
    tile_of = [
        jnp.sum(jnp.where(diagonal, tiles[d : d + 1, :], 0), axis=1, keepdims=True) for d in range(DT)
    ]
    for parity in range(2):
        picked = jnp.zeros((N_AUX, DEPTH), f32)
        for d in range(DT):
            spread = (row == d * TILE + 2 * lane + parity).astype(f32).astype(bf16)
            values = jnp.dot(coef, spread, preferred_element_type=f32)
            values = jnp.concatenate([values] * (DEPTH // 128), axis=1)
            picked = jnp.where(tile_of[d] == first, values, picked)
        for d in range(DT):
            part_rows = jnp.where(tile_of[d] == second, picked, 0.0)
            start = parity * 128 + (d % 2) * 64 + (d // 2) * 32
            chosen[start : start + 32, :] = part_rows.astype(bf16)

    virt = virt_ref[...].astype(f32)
    tile_row = lax.broadcasted_iota(jnp.int32, (NBT, TILE), 0)
    mine = lax.broadcasted_iota(jnp.int32, (1, N_AUX), 1) == me
    pieces = []
    for d in range(DT):
        tile = jnp.sum(jnp.where(mine, tiles[d : d + 1, :], 0), axis=1, keepdims=True)
        pieces.append(jnp.sum(jnp.where(tile_row == tile, virt, 0.0), axis=0, keepdims=True))
    domain = jnp.concatenate(pieces, axis=1)
    occupied = jnp.sum(jnp.where(mine, occ_ref[...].astype(f32), 0.0), axis=1, keepdims=True)
    level[...] = jnp.broadcast_to(occupied - domain, (8, WIDTH))

    low_half = lax.broadcasted_iota(jnp.int32, (64, 128), 1) < TILE

    def transform(part):
        for third in range(3):
            load(part, third).wait()

        def spread_rows(s, carry):
            for mp in range(MP):
                base = pl.multiple_of((s * MP + mp) * HALF, HALF)
                rows[pl.ds(base, HALF), :] = raw[
                    s, part * HALF : (part + 1) * HALF, mp * 128 : (mp + 1) * 128
                ].astype(f32)
            return carry

        lax.fori_loop(0, NPT, spread_rows, 0)
        matrix = chosen[...]
        for p in range(0, HALF, 2):
            panel = jnp.concatenate(
                [rows[pl.ds(p + i, DEPTH, stride=HALF), :].astype(bf16) for i in range(2)], axis=1
            )
            product = jnp.dot(matrix, panel, preferred_element_type=f32)
            for i in range(2):
                c = slice(i * 128, (i + 1) * 128)
                straight = jnp.where(low_half, product[0:64, c], product[192:256, c])
                crossed = jnp.where(low_half, product[64:128, c], product[128:192, c])
                turned[(p + i) * 64 : (p + i + 1) * 64, :] = straight + pltpu.roll(crossed, TILE, 1)
        for r in range(N_AUX):
            for pair in range(2):
                block = turned[pl.ds(pair * 32 + r, HALF, stride=64), :]
                outbox[
                    r, part * HALF : (part + 1) * HALF, pair * 128 : (pair + 1) * 128
                ] = block.astype(bf16)

    def start_sends(part):
        for k in range(1, N_AUX):
            to = behind(k)
            pltpu.make_async_remote_copy(
                src_ref=outbox.at[to, pl.ds(part * HALF, HALF)],
                dst_ref=own.at[part, k],
                send_sem=send_sem,
                recv_sem=recv_sem.at[part, k // BUNCH],
                device_id=(to, occ),
                device_id_type=MESH,
            ).start()

    def pass_level(step, target):
        return pltpu.make_async_remote_copy(
            src_ref=level, dst_ref=target, send_sem=lvl_send.at[step - 1], recv_sem=lvl_recv.at[step - 1],
            device_id=at_occ(step), device_id_type=MESH,
        )

    def bunch(ref, i):
        part, j = i // BUNCHES, i % BUNCHES
        return ref.at[part, pl.ds(j * BUNCH, BUNCH)]

    def to_next(i):
        return pltpu.make_async_remote_copy(
            src_ref=bunch(own, i), dst_ref=bunch(next1, i), send_sem=fwd_sem.at[0], recv_sem=n1_sem.at[i],
            device_id=at_occ(1), device_id_type=MESH,
        )

    def to_second(i):
        return pltpu.make_async_remote_copy(
            src_ref=bunch(own, i), dst_ref=bunch(next2, i), send_sem=fwd_sem.at[1], recv_sem=n2_sem.at[i],
            device_id=at_occ(2), device_id_type=MESH,
        )

    def relay(i):
        return pltpu.make_async_remote_copy(
            src_ref=bunch(next1, i), dst_ref=bunch(next2, i), send_sem=fwd_sem.at[2], recv_sem=n2_sem.at[i],
            device_id=at_occ(1), device_id_type=MESH,
        )

    def whole(index):
        return pltpu.make_async_remote_copy(
            src_ref=own, dst_ref=next1, send_sem=fwd_sem.at[index], recv_sem=n1_sem.at[0],
            device_id=at_occ(1), device_id_type=MESH,
        )

    def take_own(i):
        part, j = i // BUNCHES, i % BUNCHES
        k0 = max(1, j * BUNCH)
        came = own.at[part, pl.ds(k0, (j + 1) * BUNCH - k0)]
        pltpu.make_async_remote_copy(
            src_ref=came, dst_ref=came, send_sem=send_sem, recv_sem=recv_sem.at[part, j],
            device_id=at_occ(1), device_id_type=MESH,
        ).wait_recv()
        to_next(i).start()

        @pl.when(even)
        def _():
            to_second(i).start()

    def take_next(i):
        to_next(i).wait_recv()

        @pl.when(even)
        def _():
            relay(i).start()

    def take_second(i):
        to_second(i).wait_recv()

    early = my_z < NZ // 2
    transform(0)

    @pl.when(early)
    def _():
        transform(1)

    pl.semaphore_wait(barrier, N_AUX - 1 + 4)
    pass_level(1, level1).start()
    pass_level(2, level2).start()
    start_sends(0)

    @pl.when(jnp.logical_not(early))
    def _():
        transform(1)

    start_sends(1)
    keep = [pltpu.make_async_copy(outbox.at[me, pl.ds(part * HALF, HALF)], own.at[part, 0], own_sem.at[part]) for part in range(PARTS)]
    for copy in keep:
        copy.start()
    for copy in keep:
        copy.wait()
    pass_level(1, level1).wait()
    pass_level(2, level2).wait()
    column = jnp.transpose(jnp.broadcast_to(level[0:1, :], (WIDTH, WIDTH)))
    for g, other in enumerate((level, level1, level2)):
        inverse[g] = 1.0 / (column + other[0:1, :])

    def add(g, group, ref):
        part, k0 = group // 2, group % 2 * 16
        left = own[part, k0 : k0 + 16].reshape(WIDTH, WIDTH)
        right = ref[part, k0 : k0 + 16].reshape(WIDTH, WIDTH)
        product = lax.dot_general(left, right, (((0,), (0,)), ((), ())), preferred_element_type=f32)
        if group == 0:
            total[g] = product
        else:
            total[g] += product

    per_group = 2 * BUNCHES // 4

    for i in range(2 * BUNCHES):
        take_own(i)
        if i >= LAG:
            take_next(i - LAG)
        if i >= 2 * LAG:
            take_second(i - 2 * LAG)
        done = i + 1
        if done % per_group == 0:
            add(0, done // per_group - 1, own)
        done = i + 1 - LAG
        if done > 0 and done % per_group == 0:
            add(1, done // per_group - 1, next1)
        done = i + 1 - 2 * LAG
        if done > 0 and done % per_group == 0:
            add(2, done // per_group - 1, next2)
    for i in range(2 * BUNCHES - LAG, 2 * BUNCHES):
        take_next(i)
    for i in range(2 * BUNCHES - LAG, 2 * BUNCHES):
        done = i + 1
        if done % per_group == 0:
            add(1, done // per_group - 1, next1)

    def finish(g):
        value = total[g]
        ratio = value * inverse[g]
        amp_ref[g] = ratio.astype(bf16)
        energy_ref[0, g] = jnp.sum(ratio * value) / (WIDTH * WIDTH)

    finish(0)
    finish(1)
    for i in range(2 * BUNCHES - 2 * LAG, 2 * BUNCHES):
        take_second(i)
        done = i + 1
        if done % per_group == 0:
            add(2, done // per_group - 1, next2)
    finish(2)
    sent = outbox.at[pl.ds(0, N_AUX - 1)]
    pltpu.make_async_remote_copy(
        src_ref=sent, dst_ref=sent, send_sem=send_sem, recv_sem=recv_sem.at[0, 0],
        device_id=at_occ(1), device_id_type=MESH,
    ).wait_send()
    whole(0).wait_send()

    @pl.when(even)
    def _():
        whole(1).wait_send()
        whole(2).wait_send()


def per_device(integrals, tile_pairs, orbital_coef, domains, occ_energy, virt_energy):
    vmem = pl.BlockSpec(memory_space=pltpu.VMEM)
    smem = pl.BlockSpec(memory_space=pltpu.SMEM)
    amps, energies = pl.pallas_call(
        kernel,
        out_shape=(
            jax.ShapeDtypeStruct((STEPS + 1, WIDTH, WIDTH), bf16),
            jax.ShapeDtypeStruct((1, STEPS + 1), f32),
        ),
        in_specs=[pl.BlockSpec(memory_space=pltpu.HBM)] * 6,
        out_specs=(vmem, smem),
        scratch_shapes=[
            pltpu.VMEM((2, NPT), jnp.int32),
            pltpu.VMEM((N_AUX, WIDTH), bf16),
            pltpu.VMEM((DT, N_AUX), jnp.int32),
            pltpu.VMEM((1, N_AUX), bf16),
            pltpu.VMEM((NBT, TILE), bf16),
            pltpu.VMEM((NPT, AUX_DEV, TILE * TILE), bf16),
            pltpu.VMEM((DEPTH * HALF, 128), f32),
            pltpu.VMEM((HALF * 64, 128), f32),
            pltpu.VMEM((N_AUX, AUX_DEV, WIDTH), bf16),
            pltpu.VMEM((PARTS, N_AUX, HALF, WIDTH), bf16),
            pltpu.VMEM((PARTS, N_AUX, HALF, WIDTH), bf16),
            pltpu.VMEM((PARTS, N_AUX, HALF, WIDTH), bf16),
            pltpu.VMEM((256, DEPTH), bf16),
            pltpu.VMEM((8, WIDTH), f32),
            pltpu.VMEM((8, WIDTH), f32),
            pltpu.VMEM((8, WIDTH), f32),
            pltpu.VMEM((STEPS + 1, WIDTH, WIDTH), f32),
            pltpu.VMEM((STEPS + 1, WIDTH, WIDTH), f32),
            pltpu.SemaphoreType.DMA((5,)),
            pltpu.SemaphoreType.DMA((PARTS, 3)),
            pltpu.SemaphoreType.DMA((PARTS,)),
            pltpu.SemaphoreType.DMA,
            pltpu.SemaphoreType.DMA((PARTS, BUNCHES)),
            pltpu.SemaphoreType.DMA((3,)),
            pltpu.SemaphoreType.DMA((PARTS * BUNCHES,)),
            pltpu.SemaphoreType.DMA((PARTS * BUNCHES,)),
            pltpu.SemaphoreType.DMA((2,)),
            pltpu.SemaphoreType.DMA((2,)),
        ],
        compiler_params=pltpu.CompilerParams(
            collective_id=0, has_side_effects=True, vmem_limit_bytes=40 << 20
        ),
    )(
        *[
            pltpu.with_memory_space_constraint(value, pltpu.HBM)
            for value in (
                integrals,
                tile_pairs.reshape(NPT, 2).T,
                orbital_coef.reshape(N_AUX, WIDTH),
                domains.reshape(N_AUX, DT).T,
                occ_energy.T,
                virt_energy,
            )
        ]
    )
    return (
        amps.reshape(1, 1, STEPS + 1, 1, WIDTH, WIDTH),
        energies.reshape(1, 1, STEPS + 1, 1),
    )


def solution(mesh):
    in_specs = (
        P(None, "aux", None),
        P("aux", None, None),
        P(None, "occ", None),
        P(None, "occ", None),
        P(None, "occ"),
        P(),
    )
    out_specs = (P("aux", "occ", None, None, None, None), P("aux", "occ", None, None))
    return jax.shard_map(
        per_device, mesh=mesh, in_specs=in_specs, out_specs=out_specs, check_vma=False
    )
```

time: 51.1 us -> 38.2 us (0.75)
  Pallas kernels: 42.6 us -> 36.2 us
  local copies, waits for them, and re-layouts: 7.59 us -> 1.26 us
    pallas_call x1, Pallas kernels: 42.6 us -> 36.2 us  [per_device(): pl.pallas_call(kernel, out_shape=(jax.ShapeDtypeStruct((STEPS + 1, WIDTH,...]
    unnamed x11 -> x2, local copies, waits for them, and re-layouts: 6.83 us -> 1.26 us
    reshape x1 -> x0, local copies, waits for them, and re-layouts: 0.76 us -> none  [per_device(): domains.reshape(N_AUX, DT)]
where the time goes in v2:
time: 38.2 us; the launch traced here: 38.1 us
  Pallas kernels  36.2 us (95%)
  local copies, waits for them, and re-layouts  1.26 us (3%)
  between operations  0.64 us (2%)
    pallas_call x1, Pallas kernels, per_device(): pl.pallas_call(kernel, out_shape=(jax.ShapeDtypeStruct((STEPS + 1, WIDTH,...  36.2 us
    unnamed x2, local copies, waits for them, and re-layouts  1.26 us

profile of v2, /device:TPU:1, one launch (start us, length us, event | category | flops | bytes accessed | tf_op | source)
XLA Modules:
  0.0 38.1 jit_solution(5581528898675120280)
XLA Ops:
  0.6 36.2 %shard_map.77 = (bf16[3,256,256]{2,1,0:T(8,128)(2,1)S(1)}, f32[1,3]{1,0:T(1,128)S(1)}) custom-call(bf16[12,32,4096]{2,1,0:T(8,128)(2,1)} %ints_ref.1, s32[2,12]{1,0:T(2,128)} %bitcast.16, bf16[32,256]{1,0:T(8,128)(2,1)} %bitcast.14, s32[4,32]{1,0:T(4,128)} %bitcast.15, bf16[1,32]{1,0:T(2,128)(2,1)} %bitcast.17, bf16[16,64]{1,0:T(8,128)(2,1)} %virt_hbm.1), custom_call_target="tpu_custom_call" | custom-call | tf_op jit(solution)/shard_map/pallas_call | solution.py:318
  36.8 0.7 %copy.11 = bf16[1,1,3,1,256,256]{5,4,3,2,1,0:T(8,128)(2,1)} copy(bf16[1,1,3,1,256,256]{5,4,3,2,1,0:T(8,128)(2,1)S(1)} %bitcast.12) | data formatting | bytes 786432
  37.6 0.5 %copy.12 = f32[1,1,3,1]{2,3,1,0:T(1,128)} copy(f32[1,1,3,1]{2,3,1,0:T(1,128)S(1)} %bitcast.13) | data formatting | bytes 24

commit v3 on v2

--- a/solution.py
+++ b/solution.py
@@ -20,9 +20,22 @@
 DEPTH = NPT * MP
 HALF = 16
 PARTS = AUX_DEV // HALF
+SIDE = 16
 BUNCH = 4
-BUNCHES = N_AUX // BUNCH
-LAG = 4
+BUNCHES = [(0, 0, j) for j in range(0, SIDE, BUNCH)]
+BUNCHES += [(1, part, j) for part in range(PARTS) for j in range(0, SIDE, BUNCH)]
+N_FIRST = SIDE // BUNCH
+N_BUNCH = len(BUNCHES)
+ANSWER = 1
+PACE = 2
+AHEAD = 8
+LAG = 3
+LAG2 = 5
+OFFSETS = [(dx, dz) for dx in range(NX) for dz in range(NZ // 2)]
+EARLY = (tuple(range(N_BUNCH)), (10, 11))
+LATE = (tuple(range(N_FIRST, N_BUNCH)) + tuple(range(N_FIRST)), ())
+PITCH = 20
+TURN = 72
 MESH = pl.DeviceIdType.MESH
 f32 = jnp.float32
 bf16 = jnp.bfloat16
@@ -32,27 +45,41 @@
     ints_ref, pairs_hbm, coef_hbm, tiles_hbm, occ_hbm, virt_hbm,
     amp_ref, energy_ref,
     pairs_ref, coef_ref, tiles_ref, occ_ref, virt_ref,
-    raw, rows, turned, outbox, own, next1, next2, chosen, level, level1, level2, inverse, total,
-    small_sem, load_sem, own_sem, send_sem, recv_sem, fwd_sem, n1_sem, n2_sem, lvl_send, lvl_recv,
+    raw, rows, turned, outbox, own_a, own_b, next1_a, next1_b, next2_a, next2_b, chosen, level, level1, level2, inverse, total,
+    small_sem, load_sem, late_sem, send_sem, recv_sem, fwd_sem, n1_sem, n2_sem, lvl_send, lvl_recv,
 ):
     me = lax.axis_index("aux")
     occ = lax.axis_index("occ")
     my_x, my_z = me // NZ, me % NZ
     even = occ % 2 == 0
 
+    early = my_z < NZ // 2
+    late = jnp.logical_not(early)
     x_at = [lax.rem(my_x + NX - dx, NX) * NZ for dx in range(NX)]
-    z_at = [lax.rem(my_z + NZ - dz, NZ) for dz in range(NZ)]
-
-    def behind(k):
-        return x_at[k // NZ] + z_at[k % NZ]
+    z_at = [lax.rem(my_z + NZ - dz, NZ // 2) for dz in range(NZ // 2)]
+
+    def behind(side, j):
+        dx, dz = OFFSETS[j]
+        return x_at[dx] + side * (NZ // 2) + z_at[dz]
 
     def at_occ(step):
         return (me, (occ + step + N_OCC) % N_OCC)
 
     barrier = pltpu.get_barrier_semaphore()
 
-    for k in range(1, N_AUX):
-        pl.semaphore_signal(barrier, inc=1, device_id=(behind(k), occ), device_id_type=MESH)
+    def greet(side, start):
+        for j in range(start, SIDE):
+            pl.semaphore_signal(barrier, inc=1, device_id=(behind(side, j), occ), device_id_type=MESH)
+
+    @pl.when(early)
+    def _():
+        greet(0, 1)
+        greet(1, 0)
+
+    @pl.when(late)
+    def _():
+        greet(1, 1)
+
     for step in (1, 2, -1, -2):
         pl.semaphore_signal(barrier, inc=1, device_id=at_occ(step), device_id_type=MESH)
 
@@ -128,7 +155,7 @@
 
         def spread_rows(s, carry):
             for mp in range(MP):
-                base = pl.multiple_of((s * MP + mp) * HALF, HALF)
+                base = (s * MP + mp) * PITCH
                 rows[pl.ds(base, HALF), :] = raw[
                     s, part * HALF : (part + 1) * HALF, mp * 128 : (mp + 1) * 128
                 ].astype(f32)
@@ -138,32 +165,36 @@
         matrix = chosen[...]
         for p in range(0, HALF, 2):
             panel = jnp.concatenate(
-                [rows[pl.ds(p + i, DEPTH, stride=HALF), :].astype(bf16) for i in range(2)], axis=1
+                [rows[pl.ds(p + i, DEPTH, stride=PITCH), :].astype(bf16) for i in range(2)], axis=1
             )
             product = jnp.dot(matrix, panel, preferred_element_type=f32)
             for i in range(2):
                 c = slice(i * 128, (i + 1) * 128)
                 straight = jnp.where(low_half, product[0:64, c], product[192:256, c])
                 crossed = jnp.where(low_half, product[64:128, c], product[128:192, c])
-                turned[(p + i) * 64 : (p + i + 1) * 64, :] = straight + pltpu.roll(crossed, TILE, 1)
+                turned[(p + i) * TURN : (p + i) * TURN + 64, :] = straight + pltpu.roll(crossed, TILE, 1)
         for r in range(N_AUX):
             for pair in range(2):
-                block = turned[pl.ds(pair * 32 + r, HALF, stride=64), :]
+                block = turned[pl.ds(pair * 32 + r, HALF, stride=TURN), :]
                 outbox[
                     r, part * HALF : (part + 1) * HALF, pair * 128 : (pair + 1) * 128
                 ] = block.astype(bf16)
 
-    def start_sends(part):
-        for k in range(1, N_AUX):
-            to = behind(k)
-            pltpu.make_async_remote_copy(
-                src_ref=outbox.at[to, pl.ds(part * HALF, HALF)],
-                dst_ref=own.at[part, k],
-                send_sem=send_sem,
-                recv_sem=recv_sem.at[part, k // BUNCH],
-                device_id=(to, occ),
-                device_id_type=MESH,
-            ).start()
+    def send(side, same, part, js=range(SIDE)):
+        for j in js:
+            to = behind(side, j)
+            if part is None:
+                src, dst, sem = outbox.at[to], own_a.at[j], recv_sem.at[j // BUNCH]
+            else:
+                src, dst = outbox.at[to, pl.ds(part * HALF, HALF)], own_b.at[part, j]
+                sem = recv_sem.at[N_FIRST * (1 + part) + j // BUNCH]
+            if same and j == 0:
+                pltpu.make_async_copy(src, dst, sem).start()
+            else:
+                pltpu.make_async_remote_copy(
+                    src_ref=src, dst_ref=dst, send_sem=send_sem, recv_sem=sem,
+                    device_id=(to, occ), device_id_type=MESH,
+                ).start()
 
     def pass_level(step, target):
         return pltpu.make_async_remote_copy(
@@ -171,9 +202,13 @@
             device_id=at_occ(step), device_id_type=MESH,
         )
 
-    def bunch(ref, i):
-        part, j = i // BUNCHES, i % BUNCHES
-        return ref.at[part, pl.ds(j * BUNCH, BUNCH)]
+    own, next1, next2 = (own_a, own_b), (next1_a, next1_b), (next2_a, next2_b)
+
+    def bunch(refs, i):
+        which, part, j = BUNCHES[i]
+        if which == 0:
+            return refs[0].at[pl.ds(j, BUNCH)]
+        return refs[1].at[part, pl.ds(j, BUNCH)]
 
     def to_next(i):
         return pltpu.make_async_remote_copy(
@@ -193,97 +228,80 @@
             device_id=at_occ(1), device_id_type=MESH,
         )
 
-    def whole(index):
-        return pltpu.make_async_remote_copy(
-            src_ref=own, dst_ref=next1, send_sem=fwd_sem.at[index], recv_sem=n1_sem.at[0],
+    def drain(ref, sem):
+        pltpu.make_async_remote_copy(
+            src_ref=ref, dst_ref=ref, send_sem=sem, recv_sem=recv_sem.at[0],
             device_id=at_occ(1), device_id_type=MESH,
-        )
-
-    def take_own(i):
-        part, j = i // BUNCHES, i % BUNCHES
-        k0 = max(1, j * BUNCH)
-        came = own.at[part, pl.ds(k0, (j + 1) * BUNCH - k0)]
+        ).wait_send()
+
+    def take_own(i, direct):
+        came = bunch(own, i)
         pltpu.make_async_remote_copy(
-            src_ref=came, dst_ref=came, send_sem=send_sem, recv_sem=recv_sem.at[part, j],
+            src_ref=came, dst_ref=came, send_sem=send_sem, recv_sem=recv_sem.at[i],
             device_id=at_occ(1), device_id_type=MESH,
         ).wait_recv()
+        if i in direct:
+            to_second(i).start()
+        else:
+
+            @pl.when(even)
+            def _():
+                to_second(i).start()
+
         to_next(i).start()
 
-        @pl.when(even)
-        def _():
-            to_second(i).start()
-
-    def take_next(i):
+    def take_next(i, direct):
         to_next(i).wait_recv()
-
-        @pl.when(even)
-        def _():
-            relay(i).start()
+        if i not in direct:
+
+            @pl.when(even)
+            def _():
+                relay(i).start()
 
     def take_second(i):
         to_second(i).wait_recv()
 
-    early = my_z < NZ // 2
+    def send_late(i):
+        part, first_j = divmod(i * BUNCH, SIDE)
+        send(1, True, part, range(first_j, first_j + BUNCH))
+
     transform(0)
 
     @pl.when(early)
     def _():
         transform(1)
 
-    pl.semaphore_wait(barrier, N_AUX - 1 + 4)
+    pl.semaphore_wait(barrier, jnp.where(early, SIDE - 1 + 4, N_AUX - 1 + 4))
+
+    @pl.when(early)
+    def _():
+        send(0, True, None)
+
+    @pl.when(late)
+    def _():
+        for j in range(SIDE):
+            pl.semaphore_signal(late_sem, inc=1, device_id=(behind(0, j), occ), device_id_type=MESH)
+        send(0, False, 0)
+        transform(1)
+        send(0, False, 1)
+        for i in range(AHEAD):
+            send_late(i)
+
     pass_level(1, level1).start()
     pass_level(2, level2).start()
-    start_sends(0)
-
-    @pl.when(jnp.logical_not(early))
-    def _():
-        transform(1)
-
-    start_sends(1)
-    keep = [pltpu.make_async_copy(outbox.at[me, pl.ds(part * HALF, HALF)], own.at[part, 0], own_sem.at[part]) for part in range(PARTS)]
-    for copy in keep:
-        copy.start()
-    for copy in keep:
-        copy.wait()
-    pass_level(1, level1).wait()
-    pass_level(2, level2).wait()
-    column = jnp.transpose(jnp.broadcast_to(level[0:1, :], (WIDTH, WIDTH)))
-    for g, other in enumerate((level, level1, level2)):
-        inverse[g] = 1.0 / (column + other[0:1, :])
-
-    def add(g, group, ref):
-        part, k0 = group // 2, group % 2 * 16
-        left = own[part, k0 : k0 + 16].reshape(WIDTH, WIDTH)
-        right = ref[part, k0 : k0 + 16].reshape(WIDTH, WIDTH)
-        product = lax.dot_general(left, right, (((0,), (0,)), ((), ())), preferred_element_type=f32)
-        if group == 0:
-            total[g] = product
+
+    def multiply(g, refs, which, part, fresh):
+        left, right = own[which], refs[which]
+        if which == 0:
+            left, right = left[...], right[...]
         else:
-            total[g] += product
-
-    per_group = 2 * BUNCHES // 4
-
-    for i in range(2 * BUNCHES):
-        take_own(i)
-        if i >= LAG:
-            take_next(i - LAG)
-        if i >= 2 * LAG:
-            take_second(i - 2 * LAG)
-        done = i + 1
-        if done % per_group == 0:
-            add(0, done // per_group - 1, own)
-        done = i + 1 - LAG
-        if done > 0 and done % per_group == 0:
-            add(1, done // per_group - 1, next1)
-        done = i + 1 - 2 * LAG
-        if done > 0 and done % per_group == 0:
-            add(2, done // per_group - 1, next2)
-    for i in range(2 * BUNCHES - LAG, 2 * BUNCHES):
-        take_next(i)
-    for i in range(2 * BUNCHES - LAG, 2 * BUNCHES):
-        done = i + 1
-        if done % per_group == 0:
-            add(1, done // per_group - 1, next1)
+            left, right = left[part], right[part]
+        depth = left.shape[0] * left.shape[1]
+        product = lax.dot_general(
+            left.reshape(depth, WIDTH), right.reshape(depth, WIDTH),
+            (((0,), (0,)), ((), ())), preferred_element_type=f32,
+        )
+        total[g] = product if fresh else total[g] + product
 
     def finish(g):
         value = total[g]
@@ -291,25 +309,86 @@
         amp_ref[g] = ratio.astype(bf16)
         energy_ref[0, g] = jnp.sum(ratio * value) / (WIDTH * WIDTH)
 
-    finish(0)
-    finish(1)
-    for i in range(2 * BUNCHES - 2 * LAG, 2 * BUNCHES):
-        take_second(i)
-        done = i + 1
-        if done % per_group == 0:
-            add(2, done // per_group - 1, next2)
-    finish(2)
-    sent = outbox.at[pl.ds(0, N_AUX - 1)]
-    pltpu.make_async_remote_copy(
-        src_ref=sent, dst_ref=sent, send_sem=send_sem, recv_sem=recv_sem.at[0, 0],
-        device_id=at_occ(1), device_id_type=MESH,
-    ).wait_send()
-    whole(0).wait_send()
-
-    @pl.when(even)
-    def _():
-        whole(1).wait_send()
-        whole(2).wait_send()
+    def energies():
+        pass_level(1, level1).wait()
+        pass_level(2, level2).wait()
+        column = jnp.transpose(jnp.broadcast_to(level[0:1, :], (WIDTH, WIDTH)))
+        for g, other in enumerate((level, level1, level2)):
+            inverse[g] = 1.0 / (column + other[0:1, :])
+
+    def pipeline(order, direct, hook):
+        count = {}
+
+        def advance(g, refs, i):
+            which, part, _ = BUNCHES[i]
+            key = (g, which, part)
+            count[key] = count.get(key, 0) + 1
+            if count[key] == N_FIRST:
+                fresh = not any(k[0] == g and k != key and n == N_FIRST for k, n in count.items())
+                multiply(g, refs, which, part, fresh)
+
+        n = N_BUNCH
+        for step in range(n):
+            take_own(order[step], direct)
+            hook(step)
+            if step >= LAG:
+                take_next(order[step - LAG], direct)
+            if step >= LAG2:
+                take_second(order[step - LAG2])
+            if step == n - 1:
+                for back in range(LAG - 1, 0, -1):
+                    take_next(order[n - 1 - back], direct)
+            advance(0, own, order[step])
+            if step >= LAG:
+                advance(1, next1, order[step - LAG])
+            if step >= LAG2:
+                advance(2, next2, order[step - LAG2])
+            if step == LAG2:
+                energies()
+        finish(0)
+        take_next(order[n - 1], direct)
+        for back in range(LAG - 1, -1, -1):
+            advance(1, next1, order[n - 1 - back])
+        finish(1)
+        for back in range(LAG2 - 1, -1, -1):
+            take_second(order[n - 1 - back])
+            advance(2, next2, order[n - 1 - back])
+        finish(2)
+        drain(outbox.at[pl.ds(0, N_AUX - 1)], send_sem)
+        drain(own_a, fwd_sem.at[0])
+        drain(own_b, fwd_sem.at[0])
+
+        @pl.when(even)
+        def _():
+            drain(own_a, fwd_sem.at[1])
+            drain(own_b, fwd_sem.at[1])
+            for i in order:
+                if i not in direct:
+                    drain(bunch(own, i), fwd_sem.at[2])
+
+        @pl.when(jnp.logical_not(even))
+        def _():
+            for i in direct:
+                drain(bunch(own, i), fwd_sem.at[1])
+
+    @pl.when(early)
+    def _():
+        def hook(step):
+            if step == ANSWER:
+                pl.semaphore_wait(late_sem, SIDE)
+            start = (step - ANSWER) * PACE
+            if 0 <= start < SIDE:
+                send(1, False, None, range(start, start + PACE))
+
+        pipeline(*EARLY, hook)
+
+    @pl.when(late)
+    def _():
+        def hook(step):
+            if step + AHEAD < PARTS * N_FIRST:
+                send_late(step + AHEAD)
+
+        pipeline(*LATE, hook)
 
 
 def per_device(integrals, tile_pairs, orbital_coef, domains, occ_energy, virt_energy):
@@ -330,12 +409,15 @@
             pltpu.VMEM((1, N_AUX), bf16),
             pltpu.VMEM((NBT, TILE), bf16),
             pltpu.VMEM((NPT, AUX_DEV, TILE * TILE), bf16),
-            pltpu.VMEM((DEPTH * HALF, 128), f32),
-            pltpu.VMEM((HALF * 64, 128), f32),
+            pltpu.VMEM((DEPTH * PITCH, 128), f32),
+            pltpu.VMEM((HALF * TURN, 128), f32),
             pltpu.VMEM((N_AUX, AUX_DEV, WIDTH), bf16),
-            pltpu.VMEM((PARTS, N_AUX, HALF, WIDTH), bf16),
-            pltpu.VMEM((PARTS, N_AUX, HALF, WIDTH), bf16),
-            pltpu.VMEM((PARTS, N_AUX, HALF, WIDTH), bf16),
+            pltpu.VMEM((SIDE, AUX_DEV, WIDTH), bf16),
+            pltpu.VMEM((PARTS, SIDE, HALF, WIDTH), bf16),
+            pltpu.VMEM((SIDE, AUX_DEV, WIDTH), bf16),
+            pltpu.VMEM((PARTS, SIDE, HALF, WIDTH), bf16),
+            pltpu.VMEM((SIDE, AUX_DEV, WIDTH), bf16),
+            pltpu.VMEM((PARTS, SIDE, HALF, WIDTH), bf16),
             pltpu.VMEM((256, DEPTH), bf16),
             pltpu.VMEM((8, WIDTH), f32),
             pltpu.VMEM((8, WIDTH), f32),
@@ -344,12 +426,12 @@
             pltpu.VMEM((STEPS + 1, WIDTH, WIDTH), f32),
             pltpu.SemaphoreType.DMA((5,)),
             pltpu.SemaphoreType.DMA((PARTS, 3)),
-            pltpu.SemaphoreType.DMA((PARTS,)),
+            pltpu.SemaphoreType.REGULAR,
             pltpu.SemaphoreType.DMA,
-            pltpu.SemaphoreType.DMA((PARTS, BUNCHES)),
+            pltpu.SemaphoreType.DMA((N_BUNCH,)),
             pltpu.SemaphoreType.DMA((3,)),
-            pltpu.SemaphoreType.DMA((PARTS * BUNCHES,)),
-            pltpu.SemaphoreType.DMA((PARTS * BUNCHES,)),
+            pltpu.SemaphoreType.DMA((N_BUNCH,)),
+            pltpu.SemaphoreType.DMA((N_BUNCH,)),
             pltpu.SemaphoreType.DMA((2,)),
             pltpu.SemaphoreType.DMA((2,)),
         ],

time: 38.2 us -> 37.3 us (0.976)
  Pallas kernels: 36.2 us -> 35.3 us
    pallas_call x1, Pallas kernels: 36.2 us -> 35.3 us  [per_device(): pl.pallas_call(kernel, out_shape=(jax.ShapeDtypeStruct((STEPS + 1, WIDTH,...]
where the time goes in v3:
time: 37.3 us; the launch traced here: 37.2 us
  Pallas kernels  35.3 us (95%)
  local copies, waits for them, and re-layouts  1.26 us (3%)
  between operations  0.64 us (2%)
    pallas_call x1, Pallas kernels, per_device(): pl.pallas_call(kernel, out_shape=(jax.ShapeDtypeStruct((STEPS + 1, WIDTH,...  35.3 us
    unnamed x2, local copies, waits for them, and re-layouts  1.26 us

profile of v3, /device:TPU:1, one launch (start us, length us, event | category | flops | bytes accessed | tf_op | source)
XLA Modules:
  0.0 37.2 jit_solution(440580437333051160)
XLA Ops:
  0.6 35.3 %shard_map.77 = (bf16[3,256,256]{2,1,0:T(8,128)(2,1)S(1)}, f32[1,3]{1,0:T(1,128)S(1)}) custom-call(bf16[12,32,4096]{2,1,0:T(8,128)(2,1)} %ints_ref.1, s32[2,12]{1,0:T(2,128)} %bitcast.16, bf16[32,256]{1,0:T(8,128)(2,1)} %bitcast.14, s32[4,32]{1,0:T(4,128)} %bitcast.15, bf16[1,32]{1,0:T(2,128)(2,1)} %bitcast.17, bf16[16,64]{1,0:T(8,128)(2,1)} %virt_hbm.1), custom_call_target="tpu_custom_call" | custom-call | tf_op jit(solution)/shard_map/pallas_call | solution.py:397
  35.9 0.7 %copy.11 = bf16[1,1,3,1,256,256]{5,4,3,2,1,0:T(8,128)(2,1)} copy(bf16[1,1,3,1,256,256]{5,4,3,2,1,0:T(8,128)(2,1)S(1)} %bitcast.12) | data formatting | bytes 786432
  36.6 0.5 %copy.12 = f32[1,1,3,1]{2,3,1,0:T(1,128)} copy(f32[1,1,3,1]{2,3,1,0:T(1,128)S(1)} %bitcast.13) | data formatting | bytes 24

commit v4 on v3

--- a/solution.py
+++ b/solution.py
@@ -65,24 +65,6 @@
     def at_occ(step):
         return (me, (occ + step + N_OCC) % N_OCC)
 
-    barrier = pltpu.get_barrier_semaphore()
-
-    def greet(side, start):
-        for j in range(start, SIDE):
-            pl.semaphore_signal(barrier, inc=1, device_id=(behind(side, j), occ), device_id_type=MESH)
-
-    @pl.when(early)
-    def _():
-        greet(0, 1)
-        greet(1, 0)
-
-    @pl.when(late)
-    def _():
-        greet(1, 1)
-
-    for step in (1, 2, -1, -2):
-        pl.semaphore_signal(barrier, inc=1, device_id=at_occ(step), device_id_type=MESH)
-
     def load(part, third):
         s = third * 4
         return pltpu.make_async_copy(
@@ -103,6 +85,24 @@
     for part in range(PARTS):
         for third in range(3):
             load(part, third).start()
+
+    barrier = pltpu.get_barrier_semaphore()
+
+    def greet(side, start):
+        for j in range(start, SIDE):
+            pl.semaphore_signal(barrier, inc=1, device_id=(behind(side, j), occ), device_id_type=MESH)
+
+    @pl.when(early)
+    def _():
+        greet(0, 1)
+        greet(1, 0)
+
+    @pl.when(late)
+    def _():
+        greet(1, 1)
+
+    for step in (1, 2, -1, -2):
+        pl.semaphore_signal(barrier, inc=1, device_id=at_occ(step), device_id_type=MESH)
 
     for copy in small:
         copy.wait()

time: 37.3 us -> 37.2 us (level)
  Pallas kernels: 35.3 us -> 34.9 us
where the time goes in v4:
time: 37.2 us; the launch traced here: 36.8 us
  Pallas kernels  34.9 us (94%)
  local copies, waits for them, and re-layouts  1.26 us (3%)
  between operations  0.64 us (2%)
    pallas_call x1, Pallas kernels, per_device(): pl.pallas_call(kernel, out_shape=(jax.ShapeDtypeStruct((STEPS + 1, WIDTH,...  34.9 us
    unnamed x2, local copies, waits for them, and re-layouts  1.26 us

profile of v4, /device:TPU:1, one launch (start us, length us, event | category | flops | bytes accessed | tf_op | source)
XLA Modules:
  0.0 36.8 jit_solution(14679485498400424760)
XLA Ops:
  0.6 34.9 %shard_map.77 = (bf16[3,256,256]{2,1,0:T(8,128)(2,1)S(1)}, f32[1,3]{1,0:T(1,128)S(1)}) custom-call(bf16[12,32,4096]{2,1,0:T(8,128)(2,1)} %ints_ref.1, s32[2,12]{1,0:T(2,128)} %bitcast.16, bf16[32,256]{1,0:T(8,128)(2,1)} %bitcast.14, s32[4,32]{1,0:T(4,128)} %bitcast.15, bf16[1,32]{1,0:T(2,128)(2,1)} %bitcast.17, bf16[16,64]{1,0:T(8,128)(2,1)} %virt_hbm.1), custom_call_target="tpu_custom_call" | custom-call | tf_op jit(solution)/shard_map/pallas_call | solution.py:397
  35.5 0.7 %copy.11 = bf16[1,1,3,1,256,256]{5,4,3,2,1,0:T(8,128)(2,1)} copy(bf16[1,1,3,1,256,256]{5,4,3,2,1,0:T(8,128)(2,1)S(1)} %bitcast.12) | data formatting | bytes 786432
  36.3 0.5 %copy.12 = f32[1,1,3,1]{2,3,1,0:T(1,128)} copy(f32[1,1,3,1]{2,3,1,0:T(1,128)S(1)} %bitcast.13) | data formatting | bytes 24
